TPU v7x, 32 devices: a whole 2x2x4 slice. The times are simulated.
32 devices in a mesh: sec: 4 (over x, core), lat: 8 (over z, y).
Axes of the slice: x: 2, y: 2, z: 4, core: 2. Of those that a mesh axis runs over, the one named last changes fastest.
Arguments:
- ocean_state: float32 [24, 128, 1024], P(None, 'lat', 'sec'), may hold values from -6 to 6
- land_mask: int32 [128, 1024], P('lat', 'sec'), may hold values from 0 to 1
- layer_count: int32 [128, 1024], P('lat', 'sec'), may hold values from 1 to 8
- conv1_weight: bfloat16 [5, 128, 120], replicated, may hold values from -1 to 1
- conv1_bias: float32 [128], replicated, may hold values from -3 to 3
- conv2_weight: bfloat16 [5, 64, 640], replicated, may hold values from -1 to 1
- conv2_bias: float32 [64], replicated, may hold values from -3 to 3
- conv3_weight: bfloat16 [5, 32, 320], replicated, may hold values from -1 to 1
- conv3_bias: float32 [32], replicated, may hold values from -3 to 3
- conv4_weight: bfloat16 [5, 16, 160], replicated, may hold values from -1 to 1
Outputs:
- final_state: float32 [24, 128, 1024], P(None, 'lat', 'sec')
- forcing: float32 [16, 128, 1024], P(None, 'lat', 'sec')
All inputs are finite; a program needn't handle non-finite values.
Results may differ from a plain program's by a relative error of at most 0.015.
Values may be sent and summed in bfloat16 or wider, within the bound.
A program may use at most 128 MiB of HBM per device.

v0:
```python
import jax
import jax.numpy as jnp
from jax import lax
from jax.sharding import PartitionSpec as P

LEVELS = 8
STEPS = 4


time_step = 0.3
drag_rate = 0.05


def padded_2(block, sides, width):
    for axis, dim in sides:
        count = lax.axis_size(axis)
        forward = [(i, i + 1) for i in range(count - 1)]
        backward = [(target, source) for source, target in forward]
        low = lax.ppermute(
            lax.slice_in_dim(block, block.shape[dim] - width, None, axis=dim), axis, forward
        )
        high = lax.ppermute(lax.slice_in_dim(block, 0, width, axis=dim), axis, backward)
        block = jnp.concatenate([low, block, high], axis=dim)
    return block


def coupling(count_levels):
    row_index = lax.broadcasted_iota(jnp.int32, (count_levels, count_levels), 0)
    col_index = lax.broadcasted_iota(jnp.int32, (count_levels, count_levels), 1)
    return 0.5 + 0.1 * jnp.minimum(row_index, col_index).astype(jnp.float32)


def conv_layer(layer_in, weight):
    out_rows = layer_in.shape[1] - 4
    out_cols = layer_in.shape[2] - 4
    summed = jnp.zeros((weight.shape[1], out_rows, out_cols), jnp.float32)
    for shift_y in range(5):
        row_band = layer_in[:, shift_y : shift_y + out_rows, :]
        stacked = jnp.concatenate(
            [row_band[:, :, shift_x : shift_x + out_cols] for shift_x in range(5)], axis=0
        )
        summed = summed + jnp.einsum(
            "oc,crx->orx", weight[shift_y], stacked, preferred_element_type=jnp.float32
        )
    return summed


def ocean_step(padded, wet_pad, forcing, coriolis, coupling_matrix):
    zonal_vel = padded[:LEVELS]
    merid_vel = padded[LEVELS : 2 * LEVELS]
    thickness = padded[2 * LEVELS :]
    divergence = (zonal_vel[:, 1:-1, 2:] - zonal_vel[:, 1:-1, :-2]) * 0.5 + (
        merid_vel[:, 2:, 1:-1] - merid_vel[:, :-2, 1:-1]
    ) * 0.5
    h_cycle = (thickness[:, 1:-1, 1:-1] - time_step * divergence) * wet_pad[:, 1:-1, 1:-1]
    pressure = jnp.einsum("kj,jrx->krx", coupling_matrix, h_cycle, precision=lax.Precision.HIGHEST)
    grad_x = (pressure[:, 1:-1, 2:] - pressure[:, 1:-1, :-2]) * 0.5
    grad_y = (pressure[:, 2:, 1:-1] - pressure[:, :-2, 1:-1]) * 0.5
    zonal_mid = zonal_vel[:, 2:-2, 2:-2]
    merid_mid = merid_vel[:, 2:-2, 2:-2]
    wet_mid = wet_pad[:, 2:-2, 2:-2]
    zonal_new = (
        zonal_mid
        + time_step * (-grad_x + coriolis * merid_mid - drag_rate * zonal_mid + forcing[:LEVELS])
    ) * wet_mid
    merid_new = (
        merid_mid
        + time_step * (-grad_y - coriolis * zonal_mid - drag_rate * merid_mid + forcing[LEVELS:])
    ) * wet_mid
    return jnp.concatenate([zonal_new, merid_new, h_cycle[:, 1:-1, 1:-1]], axis=0)


def local(
    ocean_state,
    land_mask,
    layer_count,
    conv1_weight,
    conv1_bias,
    conv2_weight,
    conv2_bias,
    conv3_weight,
    conv3_bias,
    conv4_weight,
):
    dev_rows = ocean_state.shape[1]
    dev_cols = ocean_state.shape[2]
    row_start = lax.axis_index("lat") * dev_rows
    grid_rows = lax.axis_size("lat") * dev_rows
    levels = land_mask * layer_count
    levels_ext = padded_2(levels, (("sec", 1), ("lat", 0)), 8)
    wet_ext = (
        lax.broadcasted_iota(jnp.int32, (LEVELS, dev_rows + 16, dev_cols + 16), 0)
        < levels_ext[None]
    ).astype(jnp.float32)
    sea_ext = (levels_ext > 0).astype(jnp.float32)[None]
    wet_mask = wet_ext[:, 8:-8, 8:-8]
    wet_cycle = wet_ext[:, 6:-6, 6:-6]
    wet_two = jnp.concatenate([wet_mask, wet_mask], axis=0)
    wet_three = jnp.concatenate([wet_mask, wet_mask, wet_mask], axis=0)
    counts = jnp.maximum(lax.psum(jnp.sum(wet_mask, axis=(1, 2)), ("sec", "lat")), 1.0)
    counts_two = jnp.concatenate([counts, counts])
    global_rows = row_start + lax.broadcasted_iota(jnp.int32, (1, dev_rows, 1), 1)
    coriolis = 0.3 + 0.5 * global_rows.astype(jnp.float32) / grid_rows
    coupling_matrix = coupling(LEVELS)
    state = ocean_state * wet_three
    forcing = jnp.zeros((2 * LEVELS, dev_rows, dev_cols), jnp.float32)
    for step_index in range(STEPS):
        widened = padded_2(state.astype(jnp.bfloat16), (("sec", 2), ("lat", 1)), 8).astype(
            state.dtype
        )
        net_in = widened.astype(jnp.bfloat16)
        ocean_in = widened[:, 6:-6, 6:-6]
        hidden = net_in
        for weight, offset, margin in (
            (conv1_weight, conv1_bias, 6),
            (conv2_weight, conv2_bias, 4),
            (conv3_weight, conv3_bias, 2),
        ):
            activation = jax.nn.silu(conv_layer(hidden, weight) + offset[:, None, None])
            sea_part = sea_ext[
                :, 8 - margin : 8 + dev_rows + margin, 8 - margin : 8 + dev_cols + margin
            ]
            hidden = (activation * sea_part).astype(jnp.bfloat16)
        raw_forcing = conv_layer(hidden, conv4_weight)
        wet_sums = lax.psum(jnp.sum(raw_forcing * wet_two, axis=(1, 2)), ("sec", "lat"))
        forcing = (raw_forcing - (wet_sums / counts_two)[:, None, None]) * wet_two
        state = ocean_step(ocean_in, wet_cycle, forcing, coriolis, coupling_matrix)
    return (state, forcing)


def solution(mesh):
    return jax.shard_map(
        local,
        mesh=mesh,
        in_specs=(
            P(None, "lat", "sec"),
            P("lat", "sec"),
            P("lat", "sec"),
            P(),
            P(),
            P(),
            P(),
            P(),
            P(),
            P(),
        ),
        out_specs=(P(None, "lat", "sec"), P(None, "lat", "sec")),
        check_vma=False,
    )
```

profile of v0, /device:TPU:0, one launch (start us, length us, event | category | flops | bytes accessed | tf_op | source)
XLA Modules:
  0.0 528.2 jit_solution(6515949338046572486)
XLA Ops:
  1.4 2.3 collective-permute-start
  5.6 3.4 collective-permute-done.1
  9.1 3.4 collective-permute-start.2
  13.9 4.2 collective-permute-done.3
  20.2 2.9 collective-permute-start.4
  24.6 2.7 collective-permute-done.5
  27.5 4.3 collective-permute-start.6
  34.5 4.4 collective-permute-done.7
  48.0 2.8 fusion.16
  50.8 2.3 slice_dynamic-update-slice_fusion.79
  53.0 4.3 slice_dynamic-update-slice_fusion.78
  57.4 4.3 slice_dynamic-update-slice_fusion.77
  61.7 4.3 slice_dynamic-update-slice_fusion.76
  66.0 4.5 slice_dynamic-update-slice_fusion.75
  70.5 3.5 fusion.154
  74.0 3.5 fusion.162
  77.5 3.5 fusion.170
  81.1 3.5 fusion.178
  84.6 3.6 fusion.36
  89.0 2.1 slice_dynamic-update-slice_fusion.178
  104.4 42.2 %all-reduce = (f32[16]{0:T(128)S(1)}, f32[8]{0:T(128)S(1)}) all-reduce(f32[16]{0:T(128)S(1)} %get-tuple-element.444, f32[8]{0:T(128)S(1)} %copy-done.25), channel_id=1, replica_groups=mesh['sec'=4,'lat'=8] {'sec','lat'}, use_global_device_ids=true, to_apply=%region_1.0 | all-reduce | flops 24 | bytes 192 | tf_op jit(solution)/shard_map/psum | solution.py:125
  149.9 4.4 collective-permute-done.9
  154.5 2.4 collective-permute-start.10
  159.6 4.4 collective-permute-done.11
  173.0 2.8 fusion.17
  175.8 2.3 slice_dynamic-update-slice_fusion.54
  178.1 4.3 slice_dynamic-update-slice_fusion.53
  182.4 4.3 slice_dynamic-update-slice_fusion.52
  186.7 4.3 slice_dynamic-update-slice_fusion.51
  191.1 4.7 slice_dynamic-update-slice_fusion.50
  195.7 3.5 fusion.152
  199.2 3.5 fusion.160
  202.8 3.5 fusion.168
  206.3 3.5 fusion.176
  209.9 3.6 fusion.37
  229.4 42.8 %psum.37 = f32[16]{0:T(128)S(1)} all-reduce(f32[16]{0:T(128)S(1)} %get-tuple-element.446), channel_id=1, replica_groups=mesh['sec'=4,'lat'=8] {'sec','lat'}, use_global_device_ids=true, to_apply=%region_5.6 | all-reduce | flops 16 | bytes 128 | tf_op jit(solution)/shard_map/psum | solution.py:125
  275.5 4.4 collective-permute-done.13
  284.7 4.4 collective-permute-done.15
  298.1 3.0 fusion.18
  301.1 2.3 slice_dynamic-update-slice_fusion.29
  303.4 4.3 slice_dynamic-update-slice_fusion.28
  307.7 4.3 slice_dynamic-update-slice_fusion.27
  312.0 4.3 slice_dynamic-update-slice_fusion.26
  316.4 4.4 slice_dynamic-update-slice_fusion.25
  320.8 3.5 fusion.150
  324.3 3.5 fusion.158
  327.8 3.5 fusion.166
  331.4 3.5 fusion.174
  334.9 3.6 fusion.38
  354.5 43.5 %psum.38 = f32[16]{0:T(128)S(1)} all-reduce(f32[16]{0:T(128)S(1)} %get-tuple-element.448), channel_id=1, replica_groups=mesh['sec'=4,'lat'=8] {'sec','lat'}, use_global_device_ids=true, to_apply=%region_7.8 | all-reduce | flops 16 | bytes 128 | tf_op jit(solution)/shard_map/psum | solution.py:125
  401.2 4.4 collective-permute-done.17
  410.5 4.4 collective-permute-done.19
  425.0 2.9 fusion.19
  427.9 2.3 slice_dynamic-update-slice_fusion.4
  430.2 4.3 slice_dynamic-update-slice_fusion.3
  434.5 4.3 slice_dynamic-update-slice_fusion.2
  438.8 4.3 slice_dynamic-update-slice_fusion.1
  443.2 4.5 slice_dynamic-update-slice_fusion
  447.6 3.5 fusion.148
  451.1 3.5 fusion.156
  454.7 3.5 fusion.164
  458.2 3.5 fusion.172
  461.8 3.7 fusion.39
  481.4 43.1 %psum.39 = f32[16]{0:T(128)S(1)} all-reduce(f32[16]{0:T(128)S(1)} %get-tuple-element.450), channel_id=1, replica_groups=mesh['sec'=4,'lat'=8] {'sec','lat'}, use_global_device_ids=true, to_apply=%region_9.10 | all-reduce | flops 16 | bytes 128 | tf_op jit(solution)/shard_map/psum | solution.py:125
  (305 shorter events, 134.4 us)
Async XLA Ops:
  1.4 4.2 collective-permute-start
  3.8 5.2 collective-permute-start.1
  9.1 4.8 collective-permute-start.2
  12.5 5.6 %collective-permute-start.3 = (s32[8,272]{1,0:T(8,128)S(1)}, s32[8,272]{1,0:T(8,128)S(1)}, u32[]{:S(2)}, u32[]{:S(2)}) collective-permute-start(s32[8,272]{1,0:T(8,128)S(1)} %get-tuple-element.441), channel_id=1, source_target_pairs={{1,0},{2,1},{3,2},{4,3},{5,4},{6,5},{7,6},{9,8},{10,9},{11,10},{12... | collective-permute-start | bytes 26120 | tf_op jit(solution)/shard_map/ppermute | solution.py:22
  20.2 4.4 collective-permute-start.4
  23.1 4.2 collective-permute-start.5
  24.5 23.5 %copy-start.12 = (f32[28,268]{1,0:T(8,128)}, f32[28,268]{1,0:T(8,128)S(1)}, u32[]{:S(2)}) copy-start(f32[28,268]{1,0:T(8,128)S(1)} %slice_bitcast_fusion) | copy-start | bytes 90052
  24.6 60.0 %copy-start.19 = (f32[24,264]{1,0:T(8,128)}, f32[24,264]{1,0:T(8,128)S(1)}, u32[]{:S(2)}) copy-start(f32[24,264]{1,0:T(8,128)S(1)} %slice_bitcast_fusion.2) | copy-start | bytes 76036
  27.5 7.0 %collective-permute-start.6 = (bf16[24,8,272]{2,0,1:T(8,128)(2,1)S(1)}, bf16[24,8,272]{2,0,1:T(8,128)(2,1)S(1)}, u32[]{:S(2)}, u32[]{:S(2)}) collective-permute-start(bf16[24,8,272]{2,0,1:T(8,128)(2,1)S(1)} %get-tuple-element.430), channel_id=1, source_target_pairs={{0,1},{1,2},{2,3},{3,4},{4,5},{5,6},{6,7},{8,9},{9,10},{10,11},{11... | collective-permute-start | bytes 313352 | tf_op jit(solution)/shard_map/ppermute | solution.py:19
  31.9 7.0 %collective-permute-start.7 = (bf16[24,8,272]{2,0,1:T(8,128)(2,1)S(1)}, bf16[24,8,272]{2,0,1:T(8,128)(2,1)S(1)}, u32[]{:S(2)}, u32[]{:S(2)}) collective-permute-start(bf16[24,8,272]{2,0,1:T(8,128)(2,1)S(1)} %get-tuple-element.431), channel_id=1, source_target_pairs={{1,0},{2,1},{3,2},{4,3},{5,4},{6,5},{7,6},{9,8},{10,9},{11,10},{12... | collective-permute-start | bytes 313352 | tf_op jit(solution)/shard_map/ppermute | solution.py:22
  33.2 66.5 %copy-start.16 = (f32[20,260]{1,0:T(8,128)}, f32[20,260]{1,0:T(8,128)S(1)}, u32[]{:S(2)}) copy-start(f32[20,260]{1,0:T(8,128)S(1)} %slice_bitcast_fusion.1) | copy-start | bytes 62404
  43.5 0.9 copy-start.2
  66.0 4.5 copy-start.1
  77.5 7.1 %slice-start = ((s8[8110080]{0:T(1024)(128)(4,1)}), s8[3915776]{0:T(1024)(128)(4,1)S(1)}, s32[]{:S(2)}) async-start(s8[8110080]{0:T(1024)(128)(4,1)} %bitcast.455), calls=%async_computation | async-start | bytes 7831552
  81.0 3.5 slice-start.1
  81.0 3.5 copy-start.30
  94.4 1.7 copy-start.3
  98.8 0.9 copy-start.34
  103.4 1.0 copy-start.25
  103.7 43.1 %copy-start.23 = (f32[16]{0:T(128)S(1)}, f32[16]{0:T(128)}, u32[]{:S(2)}) copy-start(f32[16]{0:T(128)} %multiply_add_fusion.5) | copy-start | bytes 196
  103.7 43.4 %copy-start.7 = (bf16[8,16,256]{2,0,1:T(8,128)(2,1)S(1)}, bf16[8,16,256]{2,0,1:T(8,128)(2,1)}, u32[]{:S(2)}) copy-start(bf16[8,16,256]{2,0,1:T(8,128)(2,1)} %slice.4084) | copy-start | bytes 196612
  146.6 17.6 %copy-start.38 = (f32[8]{0:T(128)}, f32[8]{0:T(128)S(1)}, u32[]{:S(2)}) copy-start(f32[8]{0:T(128)S(1)} %broadcast_maximum_fusion) | copy-start | bytes 100
  147.3 2.6 collective-permute-start.8
  148.6 5.7 %collective-permute-start.9 = (bf16[24,16,8]{2,0,1:T(8,128)(2,1)S(1)}, bf16[24,16,8]{2,0,1:T(8,128)(2,1)S(1)}, u32[]{:S(2)}, u32[]{:S(2)}) collective-permute-start(bf16[24,16,8]{2,0,1:T(8,128)(2,1)S(1)} %get-tuple-element.437), channel_id=1, source_target_pairs={{8,0},{16,8},{24,16},{9,1},{17,9},{25,17},{10,2},{18,10},{26,18},{... | collective-permute-start | bytes 18440 | tf_op jit(solution)/shard_map/ppermute | solution.py:22
  154.5 5.1 collective-permute-start.10
  156.9 7.0 %collective-permute-start.11 = (bf16[24,8,272]{2,0,1:T(8,128)(2,1)S(1)}, bf16[24,8,272]{2,0,1:T(8,128)(2,1)S(1)}, u32[]{:S(2)}, u32[]{:S(2)}) collective-permute-start(bf16[24,8,272]{2,0,1:T(8,128)(2,1)S(1)} %get-tuple-element.429), channel_id=1, source_target_pairs={{1,0},{2,1},{3,2},{4,3},{5,4},{6,5},{7,6},{9,8},{10,9},{11,10},{12... | collective-permute-start | bytes 313352 | tf_op jit(solution)/shard_map/ppermute | solution.py:22
  202.8 7.1 %slice-start.2 = ((s8[8110080]{0:T(1024)(128)(4,1)}), s8[3915776]{0:T(1024)(128)(4,1)S(1)}, s32[]{:S(2)}) async-start(s8[8110080]{0:T(1024)(128)(4,1)} %bitcast.457), calls=%async_computation.2 | async-start | bytes 7831552
  206.3 3.5 slice-start.3
  206.3 3.5 copy-start.20
  206.3 3.5 copy-start.31
  219.4 1.7 copy-start.4
  223.8 0.9 copy-start.17
  223.9 0.9 copy-start.35
  228.4 43.8 %copy-start.39 = (f32[8]{0:T(128)S(1)}, f32[8]{0:T(128)}, u32[]{:S(2)}) copy-start(f32[8]{0:T(128)} %copy-done.38) | copy-start | bytes 100
  228.7 44.0 %copy-start.8 = (bf16[8,16,256]{2,0,1:T(8,128)(2,1)S(1)}, bf16[8,16,256]{2,0,1:T(8,128)(2,1)}, u32[]{:S(2)}) copy-start(bf16[8,16,256]{2,0,1:T(8,128)(2,1)} %slice.4083) | copy-start | bytes 196612
  272.8 2.6 collective-permute-start.12
  274.1 5.7 %collective-permute-start.13 = (bf16[24,16,8]{2,0,1:T(8,128)(2,1)S(1)}, bf16[24,16,8]{2,0,1:T(8,128)(2,1)S(1)}, u32[]{:S(2)}, u32[]{:S(2)}) collective-permute-start(bf16[24,16,8]{2,0,1:T(8,128)(2,1)S(1)} %get-tuple-element.435), channel_id=1, source_target_pairs={{8,0},{16,8},{24,16},{9,1},{17,9},{25,17},{10,2},{18,10},{26,18},{... | collective-permute-start | bytes 18440 | tf_op jit(solution)/shard_map/ppermute | solution.py:22
  280.1 4.6 collective-permute-start.14
  282.0 7.0 %collective-permute-start.15 = (bf16[24,8,272]{2,0,1:T(8,128)(2,1)S(1)}, bf16[24,8,272]{2,0,1:T(8,128)(2,1)S(1)}, u32[]{:S(2)}, u32[]{:S(2)}) collective-permute-start(bf16[24,8,272]{2,0,1:T(8,128)(2,1)S(1)} %get-tuple-element.427), channel_id=1, source_target_pairs={{1,0},{2,1},{3,2},{4,3},{5,4},{6,5},{7,6},{9,8},{10,9},{11,10},{12... | collective-permute-start | bytes 313352 | tf_op jit(solution)/shard_map/ppermute | solution.py:22
  327.8 7.1 %slice-start.4 = ((s8[8110080]{0:T(1024)(128)(4,1)}), s8[3915776]{0:T(1024)(128)(4,1)S(1)}, s32[]{:S(2)}) async-start(s8[8110080]{0:T(1024)(128)(4,1)} %bitcast.459), calls=%async_computation.4 | async-start | bytes 7831552
  331.4 3.5 slice-start.5
  331.4 3.5 copy-start.21
  331.4 3.5 copy-start.32
  344.5 1.7 copy-start.5
  349.0 0.9 copy-start.36
  353.5 44.5 %copy-start.40 = (f32[8]{0:T(128)S(1)}, f32[8]{0:T(128)}, u32[]{:S(2)}) copy-start(f32[8]{0:T(128)} %copy-done.38) | copy-start | bytes 100
  353.8 44.7 %copy-start.9 = (bf16[8,16,256]{2,0,1:T(8,128)(2,1)S(1)}, bf16[8,16,256]{2,0,1:T(8,128)(2,1)}, u32[]{:S(2)}) copy-start(bf16[8,16,256]{2,0,1:T(8,128)(2,1)} %slice.4082) | copy-start | bytes 196612
  398.6 2.6 collective-permute-start.16
  399.9 5.7 %collective-permute-start.17 = (bf16[24,16,8]{2,0,1:T(8,128)(2,1)S(1)}, bf16[24,16,8]{2,0,1:T(8,128)(2,1)S(1)}, u32[]{:S(2)}, u32[]{:S(2)}) collective-permute-start(bf16[24,16,8]{2,0,1:T(8,128)(2,1)S(1)} %get-tuple-element.433), channel_id=1, source_target_pairs={{8,0},{16,8},{24,16},{9,1},{17,9},{25,17},{10,2},{18,10},{26,18},{... | collective-permute-start | bytes 18440 | tf_op jit(solution)/shard_map/ppermute | solution.py:22
  405.8 4.6 collective-permute-start.18
  407.8 7.0 %collective-permute-start.19 = (bf16[24,8,272]{2,0,1:T(8,128)(2,1)S(1)}, bf16[24,8,272]{2,0,1:T(8,128)(2,1)S(1)}, u32[]{:S(2)}, u32[]{:S(2)}) collective-permute-start(bf16[24,8,272]{2,0,1:T(8,128)(2,1)S(1)} %get-tuple-element.425), channel_id=1, source_target_pairs={{1,0},{2,1},{3,2},{4,3},{5,4},{6,5},{7,6},{9,8},{10,9},{11,10},{12... | collective-permute-start | bytes 313352 | tf_op jit(solution)/shard_map/ppermute | solution.py:22
  415.1 1.0 copy-start
  424.1 0.9 copy-start.15
  424.1 0.9 copy-start.29
  454.7 7.1 %slice-start.6 = ((s8[8110080]{0:T(1024)(128)(4,1)}), s8[3915776]{0:T(1024)(128)(4,1)S(1)}, s32[]{:S(2)}) async-start(s8[8110080]{0:T(1024)(128)(4,1)} %bitcast.461), calls=%async_computation.6 | async-start | bytes 7831552
  458.2 3.5 slice-start.7
  458.2 3.5 copy-start.22
  458.2 3.5 copy-start.33
  471.5 1.7 copy-start.6
  476.0 0.9 copy-start.18
  476.0 0.9 copy-start.37
  480.4 44.1 %copy-start.41 = (f32[8]{0:T(128)S(1)}, f32[8]{0:T(128)}, u32[]{:S(2)}) copy-start(f32[8]{0:T(128)} %copy-done.38) | copy-start | bytes 100
  480.7 44.8 %copy-start.24 = (f32[16]{0:T(128)S(1)}, f32[16]{0:T(128)}, u32[]{:S(2)}) copy-start(f32[16]{0:T(128)} %multiply_add_fusion.5) | copy-start | bytes 196
  481.0 45.9 %copy-start.11 = (f32[8,16,256]{2,0,1:T(8,128)S(1)}, f32[8,16,256]{2,0,1:T(8,128)}, u32[]{:S(2)}) copy-start(f32[8,16,256]{2,0,1:T(8,128)} %slice.3102) | copy-start | bytes 393220
  (6 other events, 5.4 us)
where the time goes:
time: 536 us; the launch traced here: 528 us
  blocking collectives  172 us (32%)
  local copies, waits for them, and re-layouts  139 us (26%)
  matrix products  123 us (23%)
  waiting for transfers between devices  46.3 us (9%)
  starting transfers between devices  36.1 us (7%)
  other arithmetic  9.67 us (2%)
    psum x4, blocking collectives, local(): lax.psum(jnp.sum(raw_forcing * wet_two, axis=(1, 2)), ('sec', 'lat'))  172 us
    dot_general x80, matrix products, conv_layer(): jnp.einsum('oc,crx->orx', weight[shift_y], stacked, preferred_element_typ...  121 us
    unnamed x166, local copies, waits for them, and re-layouts  105 us
    ppermute x10, waiting for transfers between devices, padded_2(): lax.ppermute(lax.slice_in_dim(block, 0, width, axis=dim), axis, backward)  41 us
    concatenate x16, local copies, waits for them, and re-layouts, conv_layer(): jnp.concatenate([row_band[:, :, shift_x:shift_x + out_cols] for shift_x i...  29.9 us
    ppermute x10, starting transfers between devices, padded_2(): lax.ppermute(lax.slice_in_dim(block, block.shape[dim] - width, None, axis...  23.2 us
    ppermute x10, starting transfers between devices, padded_2(): lax.ppermute(lax.slice_in_dim(block, 0, width, axis=dim), axis, backward)  12.9 us
  transfers between devices with their start and end apart: 20, of which 14 were waited for; matrix products, arithmetic and copies ran while one was open for 0% of the time, Pallas kernels for 0%

commit v1 on v0

v1 whole, which is shorter than its diff:
```python
import functools

import jax
import jax.numpy as jnp
from jax import lax
from jax.experimental import pallas as pl
from jax.experimental.pallas import tpu as pltpu
from jax.sharding import PartitionSpec as P

LEVELS = 8
STEPS = 4
HALO = 8
LANES = 128
CHUNK = 512

time_step = 0.3
drag_rate = 0.05

DIRS = ((-1, 0), (1, 0), (-1, -1), (0, -1), (1, -1), (-1, 1), (0, 1), (1, 1))


def round_up(value, unit):
    return (value + unit - 1) // unit * unit


def kernel(
    rows, cols, n_sec, n_lat,
    xin, cor, cmask, w1, b1, w2, b2, w3, b3, w4,
    state_out, forcing_out,
    x, p, a1, a2, a3, raw, rawc, wet, sea,
    send_rows, send_strip, recv_rows, recv_strip, sum_sec, sum_lat, got_sec, got_lat,
    halo_send, halo_recv, sec_send, sec_recv, lat_send, lat_recv,
):
    pitch = cols + 2 * HALO
    full = (rows + 2 * HALO) * pitch
    lo, hi = HALO * pitch, (HALO + rows) * pitch
    mid = hi - lo
    sec = lax.axis_index("sec")
    lat = lax.axis_index("lat")

    exists = []
    for dl, ds in DIRS:
        ok = jnp.bool_(True)
        if dl:
            ok = jnp.logical_and(ok, lat > 0 if dl < 0 else lat < n_lat - 1)
        if ds:
            ok = jnp.logical_and(ok, sec > 0 if ds < 0 else sec < n_sec - 1)
        exists.append(ok)

    def peer(dl, ds):
        return {"sec": sec + ds, "lat": lat + dl}

    barrier = pltpu.get_barrier_semaphore()
    for d in range(1, n_sec):
        pl.semaphore_signal(
            barrier, inc=1, device_id={"sec": lax.rem(sec + d, n_sec), "lat": lat},
            device_id_type=pl.DeviceIdType.MESH,
        )
    for d in range(1, n_lat):
        pl.semaphore_signal(
            barrier, inc=1, device_id={"sec": sec, "lat": lax.rem(lat + d, n_lat)},
            device_id_type=pl.DeviceIdType.MESH,
        )
    for k, (dl, ds) in enumerate(DIRS):
        if dl and ds:

            @pl.when(exists[k])
            def _():
                pl.semaphore_signal(
                    barrier, inc=1, device_id=peer(dl, ds), device_id_type=pl.DeviceIdType.MESH
                )

    x[:, full:] = jnp.zeros((4 * LEVELS, x.shape[1] - full), jnp.float32)
    x[:, lo:hi] = xin[...]
    for k in range(len(DIRS)):

        @pl.when(jnp.logical_not(exists[k]))
        def _():
            for t in range(STEPS):
                if k < 2:
                    recv_rows[t, k] = jnp.zeros(recv_rows.shape[2:], jnp.bfloat16)
                else:
                    recv_strip[t, k - 2] = jnp.zeros(recv_strip.shape[2:], jnp.bfloat16)

    n_diag = jnp.int32(0)
    for k, (dl, ds) in enumerate(DIRS):
        if dl and ds:
            n_diag = n_diag + jnp.where(exists[k], 1, 0)
    pl.semaphore_wait(barrier, n_sec - 1 + n_lat - 1 + n_diag)

    lane = lax.broadcasted_iota(jnp.int32, (4 * LEVELS, LANES), 1)

    def halo_copy(t, k):
        dl, ds = DIRS[k]
        back = DIRS.index((-dl, -ds))
        if ds == 0:
            start = 0 if dl < 0 else mid - HALO * pitch
            src = send_rows.at[t, :, start : start + HALO * pitch]
            dst = recv_rows.at[t, back]
        else:
            src = send_strip.at[t, 0 if ds < 0 else 1]
            dst = recv_strip.at[t, back - 2]
        return pltpu.make_async_remote_copy(
            src_ref=src, dst_ref=dst, send_sem=halo_send.at[t, k], recv_sem=halo_recv.at[t, back],
            device_id=peer(dl, ds), device_id_type=pl.DeviceIdType.MESH,
        )

    def halo_arrival(t, k):
        dl, ds = DIRS[k]
        if ds == 0:
            src, dst = send_rows.at[t, :, 0 : HALO * pitch], recv_rows.at[t, k]
        else:
            src, dst = send_strip.at[t, 0], recv_strip.at[t, k - 2]
        return pltpu.make_async_remote_copy(
            src_ref=src, dst_ref=dst, send_sem=halo_send.at[t, k], recv_sem=halo_recv.at[t, k],
            device_id=peer(dl, ds), device_id_type=pl.DeviceIdType.MESH,
        )

    def start_halo(t):
        send_rows[t] = x[:, lo:hi].astype(jnp.bfloat16)
        for side in range(2):
            packed = jnp.zeros((4 * LEVELS, LANES), jnp.float32)
            for row in range(rows):
                place = (HALO + row) * pitch + (HALO if side == 0 else cols)
                base, off = place // LANES * LANES, place % LANES
                part = x[:, base : base + LANES]
                turn = (HALO * row - off) % LANES
                if turn:
                    part = pltpu.roll(part, turn, 1)
                here = (lane >= HALO * row) & (lane < HALO * (row + 1))
                packed = jnp.where(here, part, packed)
            send_strip[t, side] = packed.astype(jnp.bfloat16)
        for k in range(len(DIRS)):

            @pl.when(exists[k])
            def _():
                halo_copy(t, k).start()

    def finish_halo(t):
        for k in range(len(DIRS)):

            @pl.when(exists[k])
            def _():
                halo_arrival(t, k).wait_recv()
                halo_copy(t, k).wait_send()

        x[:, :lo] = recv_rows[t, 0].astype(jnp.float32)
        x[:, hi:full] = recv_rows[t, 1].astype(jnp.float32)
        for side in range(2):
            strips = [recv_strip[t, 3 * side + j].astype(jnp.float32) for j in range(3)]
            for ext in range(rows + 2 * HALO):
                if ext < HALO:
                    strip, from_row = strips[0], rows - HALO + ext
                elif ext < HALO + rows:
                    strip, from_row = strips[1], ext - HALO
                else:
                    strip, from_row = strips[2], ext - HALO - rows
                place = ext * pitch + (0 if side == 0 else HALO + cols)
                base, off = place // LANES * LANES, place % LANES
                turn = (off - HALO * from_row) % LANES
                if turn:
                    strip = pltpu.roll(strip, turn, 1)
                here = (lane >= off) & (lane < off + HALO)
                x[:, base : base + LANES] = jnp.where(here, strip, x[:, base : base + LANES])

    def total(t, mine):
        for axis, count, held, got, send, recv in (
            ("sec", n_sec, sum_sec, got_sec, sec_send, sec_recv),
            ("lat", n_lat, sum_lat, got_lat, lat_send, lat_recv),
        ):
            held[t] = mine
            copies = []
            for d in range(1, count):
                if axis == "sec":
                    target = {"sec": lax.rem(sec + d, count), "lat": lat}
                else:
                    target = {"sec": sec, "lat": lax.rem(lat + d, count)}
                copies.append(
                    pltpu.make_async_remote_copy(
                        src_ref=held.at[t], dst_ref=got.at[t, d - 1], send_sem=send.at[t, d - 1],
                        recv_sem=recv.at[t, d - 1], device_id=target,
                        device_id_type=pl.DeviceIdType.MESH,
                    )
                )
            for copy in copies:
                copy.start()
            for d, copy in enumerate(copies):
                copy.wait_recv()
                mine = mine + got[t, d]
            for copy in copies:
                copy.wait_send()
        counts = jnp.maximum(mine[2 * LEVELS :], 1.0)
        return (mine[: 2 * LEVELS] / jnp.concatenate([counts, counts], axis=0))[:, :1]

    def at(value, offset):
        size = value.shape[1]
        return pltpu.roll(value, (-offset) % size, 1)

    def shifted(ref, top, count, start, offset, size):
        base = offset // LANES * LANES
        rest = offset - base
        if rest == 0:
            return ref[top : top + count, pl.ds(pl.multiple_of(start + base, LANES), size)]
        wide = ref[top : top + count, pl.ds(pl.multiple_of(start + base, LANES), size + LANES)]
        return at(wide, rest)[:, :size]

    def conv(source, channels, weight, row_taps, groups, in_lanes, out_lanes, finish):
        out_channels = weight.shape[0] // groups

        def products(i, carry):
            start = i * CHUNK
            parts = [
                shifted(source, 0, channels, start, tap * pitch + s, CHUNK)
                for tap in range(row_taps)
                for s in range(5)
            ]
            stacked = jnp.concatenate(parts, axis=0).astype(jnp.bfloat16)
            p[: weight.shape[0], pl.ds(pl.multiple_of(start, LANES), CHUNK)] = jnp.dot(
                weight[...], stacked, preferred_element_type=jnp.float32
            )
            return carry

        lax.fori_loop(0, round_up(in_lanes, CHUNK) // CHUNK, products, 0)

        def reduce(i, carry):
            start = i * CHUNK
            summed = shifted(p, 0, out_channels, start, 0, CHUNK)
            for g in range(1, groups):
                summed = summed + shifted(
                    p, g * out_channels, out_channels, start, g * row_taps * pitch, CHUNK
                )
            finish(start, summed)
            return carry

        lax.fori_loop(0, round_up(out_lanes, CHUNK) // CHUNK, reduce, 0)

    def activate(layer, target, bias):
        def finish(start, summed):
            here = pl.ds(pl.multiple_of(start, LANES), CHUNK)
            value = summed + bias[...]
            half = 0.5 * value
            target[:, here] = (half + half * jnp.tanh(half)) * sea[layer, :1, here]

        return finish

    def store_raw(start, summed):
        raw[:, pl.ds(pl.multiple_of(start, LANES), CHUNK)] = summed

    def step(t, mine):
        start_halo(t)
        mean = total(t, mine)
        finish_halo(t)

        @pl.when(t == 0)
        def _():
            levels = x[3 * LEVELS :, :full]
            index = lax.broadcasted_iota(jnp.int32, (LEVELS, full), 0).astype(jnp.float32)
            wet[...] = jnp.where(index < levels, 1.0, 0.0)
            sea_here = jnp.where(levels > 0, 1.0, 0.0)
            for layer in range(3):
                sea[layer, :, :full] = at(sea_here, (layer + 1) * (2 * pitch + 2))

        for f in range(2):
            part = slice(f * LEVELS, (f + 1) * LEVELS)
            x[part, :full] = (x[part, :full] - time_step * mean[part]) * wet[...]
        x[2 * LEVELS : 3 * LEVELS, :full] = x[2 * LEVELS : 3 * LEVELS, :full] * wet[...]

        lanes = [(rows + 4 * j) * pitch for j in range(4, -1, -1)]
        conv(x, 3 * LEVELS, w1, 2, 3, lanes[0], lanes[1], activate(0, a1, b1))
        conv(a1, a1.shape[0], w2, 1, 5, lanes[1], lanes[2], activate(1, a2, b2))
        conv(a2, a2.shape[0], w3, 1, 5, lanes[2], lanes[3], activate(2, a3, b3))
        conv(a3, a3.shape[0], w4, 1, 5, lanes[3], lanes[4], store_raw)

        zonal, merid = x[:LEVELS, :full], x[LEVELS : 2 * LEVELS, :full]
        divergence = (at(zonal, 1) - at(zonal, -1)) * 0.5 + (
            at(merid, pitch) - at(merid, -pitch)
        ) * 0.5
        thick = (x[2 * LEVELS : 3 * LEVELS, :full] - time_step * divergence) * wet[...]
        level = lax.broadcasted_iota(jnp.int32, (LEVELS, 1), 0)
        pressure = jnp.zeros((LEVELS, full), jnp.float32)
        for j in range(LEVELS):
            coef = 0.5 + 0.1 * jnp.minimum(level, j).astype(jnp.float32)
            pressure = pressure + coef * thick[j : j + 1]
        grad_x = ((at(pressure, 1) - at(pressure, -1)) * 0.5)[:, lo:hi]
        grad_y = ((at(pressure, pitch) - at(pressure, -pitch)) * 0.5)[:, lo:hi]
        wet_mid = wet[:, lo:hi]
        zonal, merid = zonal[:, lo:hi], merid[:, lo:hi]
        inside = cmask[...] > 0.0
        raw_u = jnp.where(inside, pltpu.roll(raw[:LEVELS, :mid], HALO, 1), 0.0)
        raw_v = jnp.where(inside, pltpu.roll(raw[LEVELS:, :mid], HALO, 1), 0.0)
        rawc[:LEVELS] = raw_u
        rawc[LEVELS:] = raw_v
        x[:LEVELS, lo:hi] = (
            zonal + time_step * (-grad_x + cor[...] * merid - drag_rate * zonal + raw_u)
        ) * wet_mid
        x[LEVELS : 2 * LEVELS, lo:hi] = (
            merid + time_step * (-grad_y - cor[...] * zonal - drag_rate * merid + raw_v)
        ) * wet_mid
        x[2 * LEVELS : 3 * LEVELS, lo:hi] = thick[:, lo:hi]
        wet_in = jnp.where(inside, wet_mid, 0.0)
        sums = jnp.concatenate(
            [
                jnp.sum(raw_u * wet_in, axis=1, keepdims=True),
                jnp.sum(raw_v * wet_in, axis=1, keepdims=True),
                jnp.sum(wet_in, axis=1, keepdims=True),
            ],
            axis=0,
        )
        return jnp.broadcast_to(sums, (3 * LEVELS, LANES))

    mine = lax.fori_loop(0, STEPS, step, jnp.zeros((3 * LEVELS, LANES), jnp.float32))
    mean = total(STEPS, mine)
    wet_mid = wet[:, lo:hi]
    for f in range(2):
        part = slice(f * LEVELS, (f + 1) * LEVELS)
        state_out[part] = (x[part, lo:hi] - time_step * mean[part]) * wet_mid
        forcing_out[part] = (rawc[part] - mean[part]) * wet_mid
    state_out[2 * LEVELS :] = x[2 * LEVELS : 3 * LEVELS, lo:hi]


def local(
    ocean_state, land_mask, layer_count,
    conv1_weight, conv1_bias, conv2_weight, conv2_bias, conv3_weight, conv3_bias, conv4_weight,
):
    rows, cols = ocean_state.shape[1:]
    n_sec, n_lat = lax.axis_size("sec"), lax.axis_size("lat")
    pitch = cols + 2 * HALO
    full = (rows + 2 * HALO) * pitch
    mid = rows * pitch
    levels = (land_mask * layer_count).astype(jnp.float32)
    fields = jnp.concatenate(
        [ocean_state, jnp.broadcast_to(levels[None], (LEVELS, rows, cols))], axis=0
    )
    xin = jnp.pad(fields, ((0, 0), (0, 0), (HALO, HALO))).reshape(4 * LEVELS, mid)
    row = lax.broadcasted_iota(jnp.int32, (LEVELS, rows, pitch), 1)
    col = lax.broadcasted_iota(jnp.int32, (LEVELS, rows, pitch), 2)
    global_row = (lax.axis_index("lat") * rows + row).astype(jnp.float32)
    cor = (0.3 + 0.5 * global_row / (n_lat * rows)).reshape(LEVELS, mid)
    cmask = ((col >= HALO) & (col < HALO + cols)).astype(jnp.float32).reshape(LEVELS, mid)

    h1, h2, h3 = conv1_weight.shape[1], conv2_weight.shape[1], conv3_weight.shape[1]
    wide = conv1_weight.shape[2]
    w1 = jnp.pad(conv1_weight, ((0, 1), (0, 0), (0, 0))).reshape(3, 2, h1, wide)
    w1 = w1.transpose(0, 2, 1, 3).reshape(3 * h1, 2 * wide)
    w2 = conv2_weight.reshape(-1, conv2_weight.shape[2])
    w3 = conv3_weight.reshape(-1, conv3_weight.shape[2])
    w4 = conv4_weight.reshape(-1, conv4_weight.shape[2])

    room = round_up(full, CHUNK) + CHUNK
    length = [round_up((rows + 4 * j) * pitch, CHUNK) + LANES for j in (3, 2, 1)]
    most = max(w1.shape[0], w2.shape[0], w3.shape[0], w4.shape[0])
    bf, f32 = jnp.bfloat16, jnp.float32
    sums = (STEPS + 1, 3 * LEVELS, LANES)
    vmem = pl.BlockSpec(memory_space=pltpu.VMEM)
    state, forcing = pl.pallas_call(
        functools.partial(kernel, rows, cols, n_sec, n_lat),
        out_shape=(
            jax.ShapeDtypeStruct((3 * LEVELS, mid), f32),
            jax.ShapeDtypeStruct((2 * LEVELS, mid), f32),
        ),
        in_specs=[vmem] * 10,
        out_specs=(vmem, vmem),
        scratch_shapes=[
            pltpu.VMEM((4 * LEVELS, room), f32),
            pltpu.VMEM((most, room + 2 * CHUNK), f32),
            pltpu.VMEM((h1, length[0]), f32),
            pltpu.VMEM((h2, length[1]), f32),
            pltpu.VMEM((h3, length[2]), f32),
            pltpu.VMEM((2 * LEVELS, round_up(mid, CHUNK)), f32),
            pltpu.VMEM((2 * LEVELS, mid), f32),
            pltpu.VMEM((LEVELS, full), f32),
            pltpu.VMEM((3, LEVELS, room), f32),
            pltpu.VMEM((STEPS, 4 * LEVELS, mid), bf),
            pltpu.VMEM((STEPS, 2, 4 * LEVELS, LANES), bf),
            pltpu.VMEM((STEPS, 2, 4 * LEVELS, HALO * pitch), bf),
            pltpu.VMEM((STEPS, 6, 4 * LEVELS, LANES), bf),
            pltpu.VMEM(sums, f32),
            pltpu.VMEM(sums, f32),
            pltpu.VMEM((STEPS + 1, n_sec - 1) + sums[1:], f32),
            pltpu.VMEM((STEPS + 1, n_lat - 1) + sums[1:], f32),
            pltpu.SemaphoreType.DMA((STEPS, len(DIRS))),
            pltpu.SemaphoreType.DMA((STEPS, len(DIRS))),
            pltpu.SemaphoreType.DMA((STEPS + 1, n_sec - 1)),
            pltpu.SemaphoreType.DMA((STEPS + 1, n_sec - 1)),
            pltpu.SemaphoreType.DMA((STEPS + 1, n_lat - 1)),
            pltpu.SemaphoreType.DMA((STEPS + 1, n_lat - 1)),
        ],
        compiler_params=pltpu.CompilerParams(
            collective_id=0, has_side_effects=True, vmem_limit_bytes=56 * 2**20
        ),
    )(
        xin, cor, cmask,
        w1, conv1_bias[:, None], w2, conv2_bias[:, None], w3, conv3_bias[:, None], w4,
    )

    def block(flat):
        return flat.reshape(-1, rows, pitch)[:, :, HALO : HALO + cols]

    return (block(state), block(forcing))


def solution(mesh):
    return jax.shard_map(
        local,
        mesh=mesh,
        in_specs=(
            P(None, "lat", "sec"), P("lat", "sec"), P("lat", "sec"),
            P(), P(), P(), P(), P(), P(), P(),
        ),
        out_specs=(P(None, "lat", "sec"), P(None, "lat", "sec")),
        check_vma=False,
    )
```

time: 536 us -> 203 us (0.38); the launches traced: 528 us -> 202 us
  Pallas kernels: 0 us -> 189 us
  blocking collectives: 172 us -> 0 us
  local copies, waits for them, and re-layouts: 139 us -> 11.1 us
  matrix products: 123 us -> 0 us
  waiting for transfers between devices: 46.3 us -> 0 us
  starting transfers between devices: 36.1 us -> 0 us
  other arithmetic: 9.67 us -> 2.02 us
    pallas_call x0 -> x1, Pallas kernels: none -> 189 us  [local(): pl.pallas_call(functools.partial(kernel, rows, cols, n_sec, n_lat), out_s...]
    psum x4 -> x0, blocking collectives: 172 us -> none  [local(): lax.psum(jnp.sum(raw_forcing * wet_two, axis=(1, 2)), ('sec', 'lat'))]
    dot_general x84 -> x0, matrix products: 123 us -> none  [the longest x80 121 us: conv_layer(): jnp.einsum('oc,crx->orx', weight[shift_y], stacked, preferred_element_typ...]
    unnamed x166 -> x10, local copies, waits for them, and re-layouts: 105 us -> 2 us
    ppermute x20 -> x0, waiting for transfers between devices: 46.3 us -> none  [the longest x10 41 us: padded_2(): lax.ppermute(lax.slice_in_dim(block, 0, width, axis=dim), axis, backward)]
    ppermute x20 -> x0, starting transfers between devices: 36.1 us -> none  [the longest x10 23.2 us: padded_2(): lax.ppermute(lax.slice_in_dim(block, block.shape[dim] - width, None, axis...]
    concatenate x16 -> x0, local copies, waits for them, and re-layouts: 29.9 us -> none  [conv_layer(): jnp.concatenate([row_band[:, :, shift_x:shift_x + out_cols] for shift_x i...]
  transfers between devices with their start and end apart: 20 -> 0, of which waited for: 14 -> 0; matrix products, arithmetic and copies ran while one was open for 0% -> 0% of each run, Pallas kernels for 0% -> 0%
where the time goes in v1:
time: 203 us; the launch traced here: 202 us
  Pallas kernels  189 us (93%)
  local copies, waits for them, and re-layouts  11.1 us (5%)
    pallas_call x1, Pallas kernels, local(): pl.pallas_call(functools.partial(kernel, rows, cols, n_sec, n_lat), out_s...  189 us

profile of v1, /device:TPU:0, one launch (start us, length us, event | category | flops | bytes accessed | tf_op | source)
XLA Modules:
  0.0 202.4 jit_solution(13168528662627174397)
XLA Ops:
  0.6 0.7 multiply_convert_fusion
  1.4 1.3 select_maximum_fusion
  2.7 0.0 copy-start.1
  2.7 1.1 reshape.41.xin
  3.8 0.0 copy-done.1
  3.8 0.2 copy.16
  4.0 0.8 reshape.43.w1
  4.8 0.1 iota.17
  4.9 0.1 add.27
  5.0 0.7 iota.18.cor
  5.7 0.1 convert_element_type.26
  5.7 0.7 iota.21.cmask
  6.4 0.0 copy-start.2
  6.4 0.7 copy-done.2
  7.1 0.7 copy.17.b1
  7.8 0.0 copy-start.3
  7.8 0.7 copy-done.3
  8.5 0.7 copy.18.b2
  9.2 0.0 copy-start.4
  9.2 0.7 copy-done.4
  9.8 0.7 copy.19.b3
  10.5 188.5 %shard_map.113 = (f32[24,4352]{1,0:T(8,128)}, f32[16,4352]{1,0:T(8,128)}) custom-call(f32[32,4352]{1,0:T(8,128)} %reshape.41.xin, f32[8,4352]{1,0:T(8,128)} %iota.18.cor, f32[8,4352]{1,0:T(8,128)} %iota.21.cmask, bf16[384,240]{1,0:T(8,128)(2,1)} %reshape.43.w1, f32[128,1]{1,0:T(8,128)} %copy.17.b1, bf16[320,640]{1,0:T(8,128)(2,1)} %bitcast.10, ...), custom_call_target="tpu_custom_call" | custom-call | tf_op jit(solution)/shard_map/pallas_call | solution.py:355
  199.0 1.3 reshape.47
  200.4 0.0 copy-start
  200.4 0.9 slice.8
  201.3 0.0 copy-done
  201.3 0.2 reshape.48
  201.6 0.8 slice.9
  (5 shorter events, 0.0 us)
Async XLA Ops:
  2.7 1.1 copy-start.1
  6.4 0.7 copy-start.2
  7.8 0.7 copy-start.3
  9.2 0.7 copy-start.4
  200.4 1.0 copy-start

commit v2 on v1

--- a/solution.py
+++ b/solution.py
@@ -25,9 +25,9 @@
 
 def kernel(
     rows, cols, n_sec, n_lat,
-    xin, cor, cmask, w1, b1, w2, b2, w3, b3, w4,
+    xin, cor, cmask, w1_wide, b1, w2_wide, b2, w3_wide, b3, w4_wide,
     state_out, forcing_out,
-    x, p, a1, a2, a3, raw, rawc, wet, sea,
+    x, a1, a2, a3, s1, s2, s3, s4, w1, w2, w3, w4, raw, rawc, wet, sea,
     send_rows, send_strip, recv_rows, recv_strip, sum_sec, sum_lat, got_sec, got_lat,
     halo_send, halo_recv, sec_send, sec_recv, lat_send, lat_recv,
 ):
@@ -196,55 +196,140 @@
         size = value.shape[1]
         return pltpu.roll(value, (-offset) % size, 1)
 
-    def shifted(ref, top, count, start, offset, size):
-        base = offset // LANES * LANES
-        rest = offset - base
-        if rest == 0:
-            return ref[top : top + count, pl.ds(pl.multiple_of(start + base, LANES), size)]
-        wide = ref[top : top + count, pl.ds(pl.multiple_of(start + base, LANES), size + LANES)]
-        return at(wide, rest)[:, :size]
-
-    def conv(source, channels, weight, row_taps, groups, in_lanes, out_lanes, finish):
-        out_channels = weight.shape[0] // groups
-
-        def products(i, carry):
+    def shifted(ref, count, start, offset, size):
+        if offset == 0:
+            return ref[:count, pl.ds(pl.multiple_of(start, LANES), size)]
+        wide = ref[:count, pl.ds(pl.multiple_of(start, LANES), size + LANES)]
+        return at(wide, offset)[:, :size]
+
+    def band(wide, target, depth, width):
+        group = target.shape[1] // width
+        target[...] = jnp.zeros(target.shape, target.dtype)
+        for j in range(group):
+            here = slice(j * width, (j + 1) * width)
+            for r in range(5):
+                q = j + r
+                target[q * depth : (q + 1) * depth, here] = wide[r * depth : (r + 1) * depth, here]
+
+    def cells(row, offset=0, count=pitch):
+        start = pl.multiple_of(row * pitch, 16)
+        return pl.ds(start + offset if offset else start, count)
+
+    def product(source, weight, row):
+        depth = source.shape[1]
+        parts = [source[cells(row + q), :] for q in range(weight.shape[0] // depth)]
+        return jnp.dot(
+            jnp.concatenate(parts, axis=1), weight[...], preferred_element_type=jnp.float32
+        )
+
+    def silu(value):
+        half = 0.5 * value
+        return half + half * jnp.tanh(half)
+
+    def sea_row(layer, row):
+        return sea[cells(row + 2 * layer, 2 * layer), :]
+
+    lane_of = lax.broadcasted_iota(jnp.int32, (pitch, LANES), 1)
+
+    def network():
+        def gather1(i, carry):
             start = i * CHUNK
-            parts = [
-                shifted(source, 0, channels, start, tap * pitch + s, CHUNK)
-                for tap in range(row_taps)
-                for s in range(5)
+            parts = [shifted(x, 3 * LEVELS, start, s, CHUNK) for s in range(5)]
+            parts.append(jnp.zeros((LANES - 15 * LEVELS, CHUNK), jnp.float32))
+            stacked = jnp.concatenate(parts, axis=0)
+            s1[pl.ds(pl.multiple_of(start, LANES), CHUNK), :] = stacked.T.astype(jnp.bfloat16)
+            return carry
+
+        lax.fori_loop(0, s1.shape[0] // CHUNK, gather1, 0)
+
+        def conv1(g, carry):
+            row = 2 * g
+            value = silu(product(s1, w1, row) + b1[...])
+            for j in range(2):
+                a1[cells(row + j), :] = value[:, j * LANES : (j + 1) * LANES] * sea_row(1, row + j)
+            return carry
+
+        lax.fori_loop(0, (rows + 12) // 2, conv1, 0)
+
+        def gather2(row, carry):
+            for s in range(5):
+                s2[cells(row), s * LANES : (s + 1) * LANES] = a1[cells(row, s), :].astype(
+                    jnp.bfloat16
+                )
+            return carry
+
+        lax.fori_loop(0, rows + 12, gather2, 0)
+
+        def conv2(g, carry):
+            row = 4 * g
+            value = silu(product(s2, w2, row) + b2[...])
+            low = lane_of < LANES // 2
+            for k in range(2):
+                both = value[:, k * LANES : (k + 1) * LANES]
+                turned = pltpu.roll(both, LANES // 2, 1)
+                first, second = row + 2 * k, row + 2 * k + 1
+                a2[cells(first), :] = jnp.where(low, both, turned) * sea_row(2, first)
+                a2[cells(second), :] = jnp.where(low, turned, both) * sea_row(2, second)
+            return carry
+
+        lax.fori_loop(0, (rows + 8) // 4, conv2, 0)
+
+        def gather3(row, carry):
+            low = lane_of < LANES // 2
+            taps = [a2[cells(row, s), :] for s in range(5)]
+            pieces = [
+                jnp.where(low, taps[0], taps[1]), jnp.where(low, taps[2], taps[3]), taps[4],
             ]
-            stacked = jnp.concatenate(parts, axis=0).astype(jnp.bfloat16)
-            p[: weight.shape[0], pl.ds(pl.multiple_of(start, LANES), CHUNK)] = jnp.dot(
-                weight[...], stacked, preferred_element_type=jnp.float32
-            )
-            return carry
-
-        lax.fori_loop(0, round_up(in_lanes, CHUNK) // CHUNK, products, 0)
-
-        def reduce(i, carry):
-            start = i * CHUNK
-            summed = shifted(p, 0, out_channels, start, 0, CHUNK)
-            for g in range(1, groups):
-                summed = summed + shifted(
-                    p, g * out_channels, out_channels, start, g * row_taps * pitch, CHUNK
-                )
-            finish(start, summed)
-            return carry
-
-        lax.fori_loop(0, round_up(out_lanes, CHUNK) // CHUNK, reduce, 0)
-
-    def activate(layer, target, bias):
-        def finish(start, summed):
-            here = pl.ds(pl.multiple_of(start, LANES), CHUNK)
-            value = summed + bias[...]
-            half = 0.5 * value
-            target[:, here] = (half + half * jnp.tanh(half)) * sea[layer, :1, here]
-
-        return finish
-
-    def store_raw(start, summed):
-        raw[:, pl.ds(pl.multiple_of(start, LANES), CHUNK)] = summed
+            for k, piece in enumerate(pieces):
+                s3[cells(row), k * LANES : (k + 1) * LANES] = piece.astype(jnp.bfloat16)
+            return carry
+
+        lax.fori_loop(0, rows + 8, gather3, 0)
+
+        def conv3(g, carry):
+            row = 4 * g
+            value = silu(product(s3, w3, row) + b3[...])
+            for j in range(4):
+                mine = (lane_of >= 32 * j) & (lane_of < 32 * (j + 1))
+                one = jnp.where(mine, value, 0.0)
+                two = one + pltpu.roll(one, 32, 1)
+                four = two + pltpu.roll(two, 64, 1)
+                a3[cells(row + j), :] = four * sea_row(3, row + j)
+            return carry
+
+        lax.fori_loop(0, (rows + 4) // 4, conv3, 0)
+
+        def gather4(row, carry):
+            taps = [a3[cells(row, s), :] for s in range(5)]
+            piece = taps[3]
+            for j in range(3):
+                piece = jnp.where((lane_of >= 32 * j) & (lane_of < 32 * (j + 1)), taps[j], piece)
+            s4[cells(row), :LANES] = piece.astype(jnp.bfloat16)
+            s4[cells(row), LANES:] = taps[4].astype(jnp.bfloat16)
+            return carry
+
+        lax.fori_loop(0, rows + 4, gather4, 0)
+
+        value = product(s4, w4, 0)
+        tall = round_up(pitch, LANES)
+        value = jnp.concatenate(
+            [value, jnp.zeros((tall - pitch, value.shape[1]), jnp.float32)], axis=0
+        ).T
+        spot = lax.broadcasted_iota(jnp.int32, (2 * LEVELS, tall), 1)
+        for row in range(rows):
+            place = row * pitch + HALO
+            base, off = place // LANES * LANES, place % LANES
+            part = value[row * 2 * LEVELS : (row + 1) * 2 * LEVELS]
+            if off:
+                part = pltpu.roll(part, off, 1)
+            here = (spot >= off) & (spot < off + cols)
+            raw[:, base : base + tall] = jnp.where(here, part, raw[:, base : base + tall])
+
+    band(w1_wide, w1, LANES, LANES)
+    band(w2_wide, w2, 5 * LANES, LANES // 2)
+    band(w3_wide, w3, 3 * LANES, LANES // 4)
+    band(w4_wide, w4, 2 * LANES, 2 * LEVELS)
+    raw[...] = jnp.zeros(raw.shape, jnp.float32)
 
     def step(t, mine):
         start_halo(t)
@@ -257,19 +342,16 @@
             index = lax.broadcasted_iota(jnp.int32, (LEVELS, full), 0).astype(jnp.float32)
             wet[...] = jnp.where(index < levels, 1.0, 0.0)
             sea_here = jnp.where(levels > 0, 1.0, 0.0)
-            for layer in range(3):
-                sea[layer, :, :full] = at(sea_here, (layer + 1) * (2 * pitch + 2))
+            for start in range(0, full, LANES):
+                tile = jnp.concatenate([sea_here[:, start : start + LANES]] * 16, axis=0)
+                sea[start : start + LANES, :] = tile.T
 
         for f in range(2):
             part = slice(f * LEVELS, (f + 1) * LEVELS)
             x[part, :full] = (x[part, :full] - time_step * mean[part]) * wet[...]
         x[2 * LEVELS : 3 * LEVELS, :full] = x[2 * LEVELS : 3 * LEVELS, :full] * wet[...]
 
-        lanes = [(rows + 4 * j) * pitch for j in range(4, -1, -1)]
-        conv(x, 3 * LEVELS, w1, 2, 3, lanes[0], lanes[1], activate(0, a1, b1))
-        conv(a1, a1.shape[0], w2, 1, 5, lanes[1], lanes[2], activate(1, a2, b2))
-        conv(a2, a2.shape[0], w3, 1, 5, lanes[2], lanes[3], activate(2, a3, b3))
-        conv(a3, a3.shape[0], w4, 1, 5, lanes[3], lanes[4], store_raw)
+        network()
 
         zonal, merid = x[:LEVELS, :full], x[LEVELS : 2 * LEVELS, :full]
         divergence = (at(zonal, 1) - at(zonal, -1)) * 0.5 + (
@@ -286,8 +368,8 @@
         wet_mid = wet[:, lo:hi]
         zonal, merid = zonal[:, lo:hi], merid[:, lo:hi]
         inside = cmask[...] > 0.0
-        raw_u = jnp.where(inside, pltpu.roll(raw[:LEVELS, :mid], HALO, 1), 0.0)
-        raw_v = jnp.where(inside, pltpu.roll(raw[LEVELS:, :mid], HALO, 1), 0.0)
+        raw_u = jnp.where(inside, raw[:LEVELS, :mid], 0.0)
+        raw_v = jnp.where(inside, raw[LEVELS:, :mid], 0.0)
         rawc[:LEVELS] = raw_u
         rawc[LEVELS:] = raw_v
         x[:LEVELS, lo:hi] = (
@@ -338,17 +420,19 @@
     cor = (0.3 + 0.5 * global_row / (n_lat * rows)).reshape(LEVELS, mid)
     cmask = ((col >= HALO) & (col < HALO + cols)).astype(jnp.float32).reshape(LEVELS, mid)
 
-    h1, h2, h3 = conv1_weight.shape[1], conv2_weight.shape[1], conv3_weight.shape[1]
-    wide = conv1_weight.shape[2]
-    w1 = jnp.pad(conv1_weight, ((0, 1), (0, 0), (0, 0))).reshape(3, 2, h1, wide)
-    w1 = w1.transpose(0, 2, 1, 3).reshape(3 * h1, 2 * wide)
-    w2 = conv2_weight.reshape(-1, conv2_weight.shape[2])
-    w3 = conv3_weight.reshape(-1, conv3_weight.shape[2])
-    w4 = conv4_weight.reshape(-1, conv4_weight.shape[2])
-
+    def widened(weight, depth, copies):
+        turned = weight.transpose(0, 2, 1)
+        turned = jnp.pad(turned, ((0, 0), (0, depth - turned.shape[1]), (0, 0)))
+        return jnp.tile(turned.reshape(5 * depth, -1), (1, copies))
+
+    w1 = widened(conv1_weight, LANES, 2)
+    w2 = widened(conv2_weight, 5 * LANES, 4)
+    w3 = widened(conv3_weight, 3 * LANES, 4)
+    w4 = widened(conv4_weight, 2 * LANES, rows)
+    b1 = jnp.tile(conv1_bias, 2)[None]
+    b2 = jnp.tile(conv2_bias, 4)[None]
+    b3 = jnp.tile(conv3_bias, 4)[None]
     room = round_up(full, CHUNK) + CHUNK
-    length = [round_up((rows + 4 * j) * pitch, CHUNK) + LANES for j in (3, 2, 1)]
-    most = max(w1.shape[0], w2.shape[0], w3.shape[0], w4.shape[0])
     bf, f32 = jnp.bfloat16, jnp.float32
     sums = (STEPS + 1, 3 * LEVELS, LANES)
     vmem = pl.BlockSpec(memory_space=pltpu.VMEM)
@@ -362,14 +446,21 @@
         out_specs=(vmem, vmem),
         scratch_shapes=[
             pltpu.VMEM((4 * LEVELS, room), f32),
-            pltpu.VMEM((most, room + 2 * CHUNK), f32),
-            pltpu.VMEM((h1, length[0]), f32),
-            pltpu.VMEM((h2, length[1]), f32),
-            pltpu.VMEM((h3, length[2]), f32),
-            pltpu.VMEM((2 * LEVELS, round_up(mid, CHUNK)), f32),
+            pltpu.VMEM(((rows + 12) * pitch + HALO, LANES), f32),
+            pltpu.VMEM(((rows + 8) * pitch + HALO, LANES), f32),
+            pltpu.VMEM(((rows + 4) * pitch + HALO, LANES), f32),
+            pltpu.VMEM((round_up(full, CHUNK), LANES), bf),
+            pltpu.VMEM(((rows + 12) * pitch, 5 * LANES), bf),
+            pltpu.VMEM(((rows + 8) * pitch, 3 * LANES), bf),
+            pltpu.VMEM(((rows + 4) * pitch, 2 * LANES), bf),
+            pltpu.VMEM((6 * LANES, 2 * LANES), bf),
+            pltpu.VMEM((8 * 5 * LANES, 2 * LANES), bf),
+            pltpu.VMEM((8 * 3 * LANES, LANES), bf),
+            pltpu.VMEM(((rows + 4) * 2 * LANES, rows * 2 * LEVELS), bf),
+            pltpu.VMEM((2 * LEVELS, mid), f32),
             pltpu.VMEM((2 * LEVELS, mid), f32),
             pltpu.VMEM((LEVELS, full), f32),
-            pltpu.VMEM((3, LEVELS, room), f32),
+            pltpu.VMEM((full, LANES), f32),
             pltpu.VMEM((STEPS, 4 * LEVELS, mid), bf),
             pltpu.VMEM((STEPS, 2, 4 * LEVELS, LANES), bf),
             pltpu.VMEM((STEPS, 2, 4 * LEVELS, HALO * pitch), bf),
@@ -386,11 +477,11 @@
             pltpu.SemaphoreType.DMA((STEPS + 1, n_lat - 1)),
         ],
         compiler_params=pltpu.CompilerParams(
-            collective_id=0, has_side_effects=True, vmem_limit_bytes=56 * 2**20
+            collective_id=0, has_side_effects=True, vmem_limit_bytes=60 * 2**20
         ),
     )(
         xin, cor, cmask,
-        w1, conv1_bias[:, None], w2, conv2_bias[:, None], w3, conv3_bias[:, None], w4,
+        w1, b1, w2, b2, w3, b3, w4,
     )
 
     def block(flat):

time: 203 us -> 165 us (0.81)
  Pallas kernels: 189 us -> 148 us
  local copies, waits for them, and re-layouts: 11.1 us -> 14.8 us
    pallas_call x1, Pallas kernels: 189 us -> 148 us  [local(): pl.pallas_call(functools.partial(kernel, rows, cols, n_sec, n_lat), out_s...]
    another operation x0 -> x13, local copies, waits for them, and re-layouts: none -> 7.71 us  [the longest x8 5.78 us: widened(): return jnp.tile(turned.reshape(5 * depth, -1), (1, copies))]
    broadcast_in_dim x3 -> x0, local copies, waits for them, and re-layouts: 2.1 us -> none  [the longest x1 0.73 us: local(): conv1_bias[:, None]]
where the time goes in v2:
time: 165 us; the launch traced here: 164 us
  Pallas kernels  148 us (90%)
  local copies, waits for them, and re-layouts  14.8 us (9%)
    pallas_call x1, Pallas kernels, local(): pl.pallas_call(functools.partial(kernel, rows, cols, n_sec, n_lat), out_s...  148 us
    another operation x8, local copies, waits for them, and re-layouts, widened(): return jnp.tile(turned.reshape(5 * depth, -1), (1, copies))  5.78 us

profile of v2, /device:TPU:0, one launch (start us, length us, event | category | flops | bytes accessed | tf_op | source)
XLA Modules:
  0.0 164.4 jit_solution(14164673782230369870)
XLA Ops:
  0.6 1.0 copy.20
  1.7 0.1 tile.63
  1.8 0.0 copy-start.3
  1.8 2.3 %copy.15.w2_wide = bf16[3200,256]{1,0:T(8,128)(2,1)} copy(bf16[3200,256]{0,1:T(8,128)(2,1)S(1)} %bitcast.23) | data formatting | bytes 3276800 | tf_op jit(solution)/shard_map/tile | solution.py:426
  4.1 0.0 copy-start.5
  4.1 0.0 copy-start.6
  4.1 0.0 copy-start
  4.1 0.0 copy-done.3
  4.1 0.1 copy.18
  4.3 1.0 copy.16.w3_wide
  5.3 0.0 copy-done.5
  5.3 0.0 copy-done.6
  5.3 0.0 copy-start.4
  5.3 0.0 copy-done
  5.3 0.3 select_maximum_fusion
  5.6 0.0 copy-start.2
  5.6 1.1 reshape.45.xin
  6.7 0.0 copy-done.4
  6.8 0.0 copy-start.7
  6.9 0.0 copy-start.8
  6.9 0.0 copy-start.9
  6.9 1.1 copy.17.w4_wide
  8.0 0.0 copy-done.2
  8.0 0.2 tile.59
  8.2 0.8 copy.25
  9.0 0.1 iota.17
  9.0 0.1 add.31
  9.1 0.7 iota.18.cor
  9.8 0.1 convert_element_type.30
  9.9 0.7 iota.21.cmask
  10.5 0.0 copy-done.7
  10.6 0.7 broadcast_in_dim_tile.10.b2
  11.2 0.0 copy-done.8
  11.2 0.7 broadcast_in_dim_tile.11.b3
  11.9 0.0 copy-done.9
  11.9 0.6 tile.61
  12.5 148.5 %shard_map.113 = (f32[24,4352]{1,0:T(8,128)}, f32[16,4352]{1,0:T(8,128)}) custom-call(f32[32,4352]{1,0:T(8,128)} %reshape.45.xin, f32[8,4352]{1,0:T(8,128)} %iota.18.cor, f32[8,4352]{1,0:T(8,128)} %iota.21.cmask, bf16[640,256]{1,0:T(8,128)(2,1)} %bitcast.28, f32[1,256]{1,0:T(1,128)} %bitcast.38, bf16[3200,256]{1,0:T(8,128)(2,1)} %copy.15.w2_wide, ...), custom_call_target="tpu_custom_call" | custom-call | tf_op jit(solution)/shard_map/pallas_call | solution.py:439
  161.0 0.0 copy-start.1
  161.0 1.4 reshape.46
  162.4 0.9 slice.8
  163.3 0.0 copy-done.1
  163.3 0.2 reshape.47
  163.5 0.8 slice.9
  (15 shorter events, 0.2 us)
Async XLA Ops:
  1.8 2.3 %copy-start.3 = (bf16[5,32,320]{2,1,0:T(8,128)(2,1)S(1)}, bf16[5,32,320]{2,1,0:T(8,128)(2,1)}, u32[]{:S(2)}) copy-start(bf16[5,32,320]{2,1,0:T(8,128)(2,1)} %param.17) | copy-start | bytes 307204
  4.1 1.2 copy-start.5
  4.1 1.2 copy-start.6
  4.1 1.2 copy-start
  5.3 1.4 copy-start.4
  5.6 2.4 %copy-start.2 = (bf16[5,128,120]{1,2,0:T(8,128)(2,1)S(1)}, bf16[5,128,120]{1,2,0:T(8,128)(2,1)}, u32[]{:S(2)}) copy-start(bf16[5,128,120]{1,2,0:T(8,128)(2,1)} %param.13) | copy-start | bytes 460804
  6.8 3.7 %copy-start.7 = (f32[64]{0:T(128)S(1)}, f32[64]{0:T(128)}, u32[]{:S(2)}) copy-start(f32[64]{0:T(128)} %param.16) | copy-start | bytes 772
  6.9 4.4 %copy-start.8 = (f32[32]{0:T(128)S(1)}, f32[32]{0:T(128)}, u32[]{:S(2)}) copy-start(f32[32]{0:T(128)} %param.18) | copy-start | bytes 388
  6.9 5.0 %copy-start.9 = (f32[128]{0:T(128)S(1)}, f32[128]{0:T(128)}, u32[]{:S(2)}) copy-start(f32[128]{0:T(128)} %param.14) | copy-start | bytes 1540
  161.0 2.3 %copy-start.1 = (f32[16,4352]{1,0:T(8,128)S(1)}, f32[16,4352]{1,0:T(8,128)}, u32[]{:S(2)}) copy-start(f32[16,4352]{1,0:T(8,128)} %get-tuple-element.5) | copy-start | bytes 835588

commit v3 on v2

--- a/solution.py
+++ b/solution.py
@@ -25,9 +25,9 @@
 
 def kernel(
     rows, cols, n_sec, n_lat,
-    xin, cor, cmask, w1_wide, b1, w2_wide, b2, w3_wide, b3, w4_wide,
+    xin, w1_wide, b1, w2_wide, b2, w3_wide, b3, w4_wide,
     state_out, forcing_out,
-    x, a1, a2, a3, s1, s2, s3, s4, w1, w2, w3, w4, raw, rawc, wet, sea,
+    x, a1, a2, a3, s1, s2, s3, s4, w1, w2, w3, w4, raw, rawc, wet, sea, cor, cmask,
     send_rows, send_strip, recv_rows, recv_strip, sum_sec, sum_lat, got_sec, got_lat,
     halo_send, halo_recv, sec_send, sec_recv, lat_send, lat_recv,
 ):
@@ -229,6 +229,16 @@
     def sea_row(layer, row):
         return sea[cells(row + 2 * layer, 2 * layer), :]
 
+    def loop(count, body, several):
+        several = several if count % several == 0 else 1
+
+        def some(i, carry):
+            for j in range(several):
+                body(i * several + j, carry)
+            return carry
+
+        lax.fori_loop(0, count // several, some, 0)
+
     lane_of = lax.broadcasted_iota(jnp.int32, (pitch, LANES), 1)
 
     def network():
@@ -249,7 +259,7 @@
                 a1[cells(row + j), :] = value[:, j * LANES : (j + 1) * LANES] * sea_row(1, row + j)
             return carry
 
-        lax.fori_loop(0, (rows + 12) // 2, conv1, 0)
+        loop((rows + 12) // 2, conv1, 2)
 
         def gather2(row, carry):
             for s in range(5):
@@ -258,7 +268,7 @@
                 )
             return carry
 
-        lax.fori_loop(0, rows + 12, gather2, 0)
+        loop(rows + 12, gather2, 2)
 
         def conv2(g, carry):
             row = 4 * g
@@ -272,7 +282,7 @@
                 a2[cells(second), :] = jnp.where(low, turned, both) * sea_row(2, second)
             return carry
 
-        lax.fori_loop(0, (rows + 8) // 4, conv2, 0)
+        loop((rows + 8) // 4, conv2, 2)
 
         def gather3(row, carry):
             low = lane_of < LANES // 2
@@ -284,7 +294,7 @@
                 s3[cells(row), k * LANES : (k + 1) * LANES] = piece.astype(jnp.bfloat16)
             return carry
 
-        lax.fori_loop(0, rows + 8, gather3, 0)
+        loop(rows + 8, gather3, 2)
 
         def conv3(g, carry):
             row = 4 * g
@@ -297,7 +307,7 @@
                 a3[cells(row + j), :] = four * sea_row(3, row + j)
             return carry
 
-        lax.fori_loop(0, (rows + 4) // 4, conv3, 0)
+        loop((rows + 4) // 4, conv3, 5)
 
         def gather4(row, carry):
             taps = [a3[cells(row, s), :] for s in range(5)]
@@ -308,7 +318,7 @@
             s4[cells(row), LANES:] = taps[4].astype(jnp.bfloat16)
             return carry
 
-        lax.fori_loop(0, rows + 4, gather4, 0)
+        loop(rows + 4, gather4, 2)
 
         value = product(s4, w4, 0)
         tall = round_up(pitch, LANES)
@@ -330,6 +340,18 @@
     band(w3_wide, w3, 3 * LANES, LANES // 4)
     band(w4_wide, w4, 2 * LANES, 2 * LEVELS)
     raw[...] = jnp.zeros(raw.shape, jnp.float32)
+
+    def places():
+        spot = lax.broadcasted_iota(jnp.int32, (LEVELS, mid), 1)
+        row = jnp.zeros((LEVELS, mid), jnp.int32)
+        for k in range(1, rows):
+            row = row + jnp.where(spot >= k * pitch, 1, 0)
+        col = spot - row * pitch
+        global_row = (lat * rows + row).astype(jnp.float32)
+        cor[...] = 0.3 + 0.5 * global_row / (n_lat * rows)
+        cmask[...] = jnp.where((col >= HALO) & (col < HALO + cols), 1.0, 0.0)
+
+    places()
 
     def step(t, mine):
         start_halo(t)
@@ -414,12 +436,6 @@
         [ocean_state, jnp.broadcast_to(levels[None], (LEVELS, rows, cols))], axis=0
     )
     xin = jnp.pad(fields, ((0, 0), (0, 0), (HALO, HALO))).reshape(4 * LEVELS, mid)
-    row = lax.broadcasted_iota(jnp.int32, (LEVELS, rows, pitch), 1)
-    col = lax.broadcasted_iota(jnp.int32, (LEVELS, rows, pitch), 2)
-    global_row = (lax.axis_index("lat") * rows + row).astype(jnp.float32)
-    cor = (0.3 + 0.5 * global_row / (n_lat * rows)).reshape(LEVELS, mid)
-    cmask = ((col >= HALO) & (col < HALO + cols)).astype(jnp.float32).reshape(LEVELS, mid)
-
     def widened(weight, depth, copies):
         turned = weight.transpose(0, 2, 1)
         turned = jnp.pad(turned, ((0, 0), (0, depth - turned.shape[1]), (0, 0)))
@@ -442,7 +458,7 @@
             jax.ShapeDtypeStruct((3 * LEVELS, mid), f32),
             jax.ShapeDtypeStruct((2 * LEVELS, mid), f32),
         ),
-        in_specs=[vmem] * 10,
+        in_specs=[vmem] * 8,
         out_specs=(vmem, vmem),
         scratch_shapes=[
             pltpu.VMEM((4 * LEVELS, room), f32),
@@ -461,6 +477,8 @@
             pltpu.VMEM((2 * LEVELS, mid), f32),
             pltpu.VMEM((LEVELS, full), f32),
             pltpu.VMEM((full, LANES), f32),
+            pltpu.VMEM((LEVELS, mid), f32),
+            pltpu.VMEM((LEVELS, mid), f32),
             pltpu.VMEM((STEPS, 4 * LEVELS, mid), bf),
             pltpu.VMEM((STEPS, 2, 4 * LEVELS, LANES), bf),
             pltpu.VMEM((STEPS, 2, 4 * LEVELS, HALO * pitch), bf),
@@ -480,7 +498,7 @@
             collective_id=0, has_side_effects=True, vmem_limit_bytes=60 * 2**20
         ),
     )(
-        xin, cor, cmask,
+        xin,
         w1, b1, w2, b2, w3, b3, w4,
     )
 

time: 165 us -> 154 us (0.933)
  Pallas kernels: 148 us -> 139 us
  local copies, waits for them, and re-layouts: 14.8 us -> 13.1 us
    pallas_call x1, Pallas kernels: 148 us -> 139 us  [local(): pl.pallas_call(functools.partial(kernel, rows, cols, n_sec, n_lat), out_s...]
where the time goes in v3:
time: 154 us
  Pallas kernels  139 us (90%)
  local copies, waits for them, and re-layouts  13.1 us (9%)
    pallas_call x1, Pallas kernels, local(): pl.pallas_call(functools.partial(kernel, rows, cols, n_sec, n_lat), out_s...  139 us
    another operation x8, local copies, waits for them, and re-layouts, widened(): return jnp.tile(turned.reshape(5 * depth, -1), (1, copies))  5.78 us

profile of v3, /device:TPU:0, one launch (start us, length us, event | category | flops | bytes accessed | tf_op | source)
XLA Modules:
  0.0 153.7 jit_solution(13080285472673584849)
XLA Ops:
  0.6 1.0 copy.20
  1.7 0.1 tile.63
  1.8 0.0 copy-start.3
  1.8 2.3 %copy.15.w2_wide = bf16[3200,256]{1,0:T(8,128)(2,1)} copy(bf16[3200,256]{0,1:T(8,128)(2,1)S(1)} %bitcast.23) | data formatting | bytes 3276800 | tf_op jit(solution)/shard_map/tile | solution.py:442
  4.1 0.0 copy-start.5
  4.1 0.0 copy-start.6
  4.1 0.0 copy-start
  4.1 0.0 copy-done.3
  4.1 0.1 copy.18
  4.3 1.0 copy.16.w3_wide
  5.3 0.0 copy-done.5
  5.3 0.0 copy-done.6
  5.3 0.0 copy-start.4
  5.3 0.0 copy-done
  5.3 0.3 select_maximum_fusion
  5.6 0.0 copy-start.2
  5.6 1.1 reshape.33.xin
  6.7 0.0 copy-done.4
  6.8 0.0 copy-start.7
  6.8 0.0 copy-start.8
  6.8 0.0 copy-start.9
  6.9 1.1 copy.17.w4_wide
  8.0 0.0 copy-done.2
  8.0 0.2 tile.59
  8.2 0.8 copy.25
  8.9 0.0 copy-done.7
  9.0 0.7 broadcast_in_dim_tile.10.b2
  9.6 0.0 copy-done.8
  9.6 0.6 broadcast_in_dim_tile.11.b3
  10.2 0.0 copy-done.9
  10.2 0.6 tile.61
  10.8 139.5 %shard_map.113 = (f32[24,4352]{1,0:T(8,128)}, f32[16,4352]{1,0:T(8,128)}) custom-call(f32[32,4352]{1,0:T(8,128)} %reshape.33.xin, bf16[640,256]{1,0:T(8,128)(2,1)} %bitcast.27, f32[1,256]{1,0:T(1,128)} %bitcast.38, bf16[3200,256]{1,0:T(8,128)(2,1)} %copy.15.w2_wide, f32[1,256]{1,0:T(1,128)} %broadcast_in_dim_tile.10.b2, bf16[1920,128]{1,0:T(8,128)(2,1)} %copy.16.w3_wide, ...), custom_call_target="tpu_custom_call" | custom-call | tf_op jit(solution)/shard_map/pallas_call | solution.py:455
  150.3 0.0 copy-start.1
  150.3 1.4 reshape.34
  151.7 0.9 slice.8
  152.6 0.0 copy-done.1
  152.6 0.2 reshape.35
  152.8 0.8 slice.9
  (12 shorter events, 0.2 us)
Async XLA Ops:
  1.8 2.3 %copy-start.3 = (bf16[5,32,320]{2,1,0:T(8,128)(2,1)S(1)}, bf16[5,32,320]{2,1,0:T(8,128)(2,1)}, u32[]{:S(2)}) copy-start(bf16[5,32,320]{2,1,0:T(8,128)(2,1)} %param.17) | copy-start | bytes 307204
  4.1 1.2 copy-start.5
  4.1 1.2 copy-start.6
  4.1 1.2 copy-start
  5.3 1.4 copy-start.4
  5.6 2.4 %copy-start.2 = (bf16[5,128,120]{1,2,0:T(8,128)(2,1)S(1)}, bf16[5,128,120]{1,2,0:T(8,128)(2,1)}, u32[]{:S(2)}) copy-start(bf16[5,128,120]{1,2,0:T(8,128)(2,1)} %param.13) | copy-start | bytes 460804
  6.8 2.2 %copy-start.7 = (f32[64]{0:T(128)S(1)}, f32[64]{0:T(128)}, u32[]{:S(2)}) copy-start(f32[64]{0:T(128)} %param.16) | copy-start | bytes 772
  6.8 2.8 %copy-start.8 = (f32[32]{0:T(128)S(1)}, f32[32]{0:T(128)}, u32[]{:S(2)}) copy-start(f32[32]{0:T(128)} %param.18) | copy-start | bytes 388
  6.8 3.4 %copy-start.9 = (f32[128]{0:T(128)S(1)}, f32[128]{0:T(128)}, u32[]{:S(2)}) copy-start(f32[128]{0:T(128)} %param.14) | copy-start | bytes 1540
  150.3 2.3 %copy-start.1 = (f32[16,4352]{1,0:T(8,128)S(1)}, f32[16,4352]{1,0:T(8,128)}, u32[]{:S(2)}) copy-start(f32[16,4352]{1,0:T(8,128)} %get-tuple-element.5) | copy-start | bytes 835588
